TPU v7x, 32 devices: a whole 2x2x4 slice. The times are simulated.
32 devices in a mesh: gx: 4 (over x, core), gy: 8 (over z, y).
Axes of the slice: x: 2, y: 2, z: 4, core: 2. Of those that a mesh axis runs over, the one named last changes fastest.
Arguments:
- chi: float32 [32, 32, 256], P('gy', 'gx'), may hold values from -6 to 6
- sigma: float32 [32, 32, 256], P('gy', 'gx'), may hold values from 25 to 250
- vertical: float32 [4, 64, 64], replicated, may hold values from -0.75 to 0.75
- kx: float32 [32, 32, 256], P('gy', 'gx'), may hold values from 4 to 120
- ky: float32 [32, 32, 256], P('gy', 'gx'), may hold values from 256 to 7680
Outputs:
- increment: float32 [32, 32, 256], P('gy', 'gx')
All inputs are finite; a program needn't handle non-finite values.
Results may differ from a plain program's by a relative error of at most 0.0003.
Values sent between devices are 32-bit elements; how exact they have to be, the bound alone decides.
A program may use at most 64 MiB of HBM per device.

v0:
```python
import functools

import jax
import jax.numpy as jnp
from jax import lax
from jax.experimental import pallas as pl
from jax.experimental.pallas import tpu as pltpu
from jax.sharding import PartitionSpec as P

ITERS = 3


def mobius_join(earlier, later):
    top_left = later[0] * earlier[0] + later[1] * earlier[2]
    top_right = later[0] * earlier[1] + later[1] * earlier[3]
    low_left = later[2] * earlier[0] + later[3] * earlier[2]
    low_right = later[2] * earlier[1] + later[3] * earlier[3]
    factor = 1.0 / (top_left + top_right + low_left + low_right)
    return (top_left * factor, top_right * factor, low_left * factor, low_right * factor)


def affine_join(earlier, later):
    return (earlier[0] * later[0], later[0] * earlier[1] + later[1])


def mobius_value(matrix):
    return (matrix[0] + matrix[1]) / (matrix[2] + matrix[3])


def neutral(sample):
    filled = jnp.ones_like(sample[0])
    emptied = jnp.zeros_like(sample[0])
    if len(sample) == 4:
        return (filled, emptied, emptied, filled)
    return (filled, emptied)


def settle(gathered, split, join, position):
    ups = tuple((gathered[:, member_id] for member_id in range(split)))
    downs = tuple((gathered[:, member_id] for member_id in range(split, gathered.shape[1])))
    up_scan = lax.associative_scan(join, ups, axis=0)
    down_scan = lax.associative_scan(join, downs, reverse=True, axis=0)
    up_open = neutral(tuple((member[0] for member in ups)))
    down_open = neutral(tuple((member[0] for member in downs)))
    up_in = tuple(
        (
            lax.dynamic_index_in_dim(jnp.concatenate([anchor[None], member], 0), position, 0, False)
            for anchor, member in zip(up_open, up_scan)
        )
    )
    down_in = tuple(
        (
            lax.dynamic_index_in_dim(
                jnp.concatenate([member, anchor[None]], 0), position + 1, 0, False
            )
            for anchor, member in zip(down_open, down_scan)
        )
    )
    return (up_in, down_in)


def across_x(up_total, down_total, join):
    packed = jnp.stack(up_total + down_total, 0)[None]
    gathered = lax.all_gather(packed, "gx", axis=0, tiled=True)
    return settle(gathered, len(up_total), join, lax.axis_index("gx"))


def across_y(up_total, down_total, join):
    up_in = neutral(up_total)
    down_in = neutral(down_total)
    return (up_in, down_in)


def chain(up_elements, down_elements, join, axis_dim, across):
    span = up_elements[0].shape[axis_dim]
    up_local = lax.associative_scan(join, up_elements, axis=axis_dim)
    down_local = lax.associative_scan(join, down_elements, reverse=True, axis=axis_dim)
    up_total = tuple((lax.index_in_dim(member, span - 1, axis_dim, False) for member in up_local))
    down_total = tuple((lax.index_in_dim(member, 0, axis_dim, False) for member in down_local))
    up_in, down_in = across(up_total, down_total, join)
    up_whole = join(tuple((jnp.expand_dims(member, axis_dim) for member in up_in)), up_local)
    down_whole = join(tuple((jnp.expand_dims(member, axis_dim) for member in down_in)), down_local)
    return (up_in, up_whole, down_in, down_whole)


def open_edge(conduct, axis_dim, position):
    span = conduct.shape[axis_dim]
    place = lax.broadcasted_iota(jnp.int32, conduct.shape, axis_dim) + position * span
    return jnp.where(place == 0, jnp.zeros_like(conduct), conduct)


def operator_terms(kleft, axis_dim, across):
    span = kleft.shape[axis_dim]
    matrices = (1.0 + kleft, kleft, jnp.ones_like(kleft), kleft)
    up_in, up_whole, down_in, down_whole = chain(matrices, matrices, mobius_join, axis_dim, across)
    after = mobius_value(up_whole)
    before = jnp.concatenate(
        [
            jnp.expand_dims(mobius_value(up_in), axis_dim),
            lax.slice_in_dim(after, 0, span - 1, 1, axis_dim),
        ],
        axis_dim,
    )
    behind_whole = mobius_value(down_whole)
    behind = jnp.concatenate(
        [
            lax.slice_in_dim(behind_whole, 1, span, 1, axis_dim),
            jnp.expand_dims(mobius_value(down_in), axis_dim),
        ],
        axis_dim,
    )
    return (kleft / (before + kleft), kleft / (behind + kleft), after + behind - 1.0)


def line_solve(values, terms, axis_dim, across):
    forward_rate, backward_rate, diagonal = terms
    span = values.shape[axis_dim]
    up_in, up_whole, down_in, down_whole = chain(
        (forward_rate, values),
        (backward_rate, backward_rate * values),
        affine_join,
        axis_dim,
        across,
    )
    passed = down_whole[1]
    passed_next = jnp.concatenate(
        [lax.slice_in_dim(passed, 1, span, 1, axis_dim), jnp.expand_dims(down_in[1], axis_dim)],
        axis_dim,
    )
    return (up_whole[1] + passed_next) / diagonal


def to_lines(field, partners):
    row_count = field.shape[0]
    flattened = field.reshape(row_count, -1)
    padding = -flattened.shape[1] % partners
    return jnp.pad(flattened, ((0, 0), (0, padding)))


def from_lines(lines, target_shape):
    return lines[:, : target_shape[1] * target_shape[2]].reshape(target_shape)


def body(chi, sigma, vertical, kx, ky):
    fields = vertical.shape[0]
    levels = vertical.shape[1]
    width = fields * levels
    scaled = sigma * chi
    blocks = (
        jnp.eye(fields, dtype=jnp.float32)[:, None, :, None] * vertical[:, :, None, :]
    ).reshape(width, width)
    mixed = jnp.dot(scaled.reshape(-1, width), blocks, precision=lax.Precision.HIGHEST).reshape(
        scaled.shape
    )
    x_terms = operator_terms(open_edge(kx, 1, lax.axis_index("gx")), 1, across_x)
    partners = lax.axis_size("gy")
    whole_conduct = lax.all_to_all(
        to_lines(ky, partners), "gy", split_axis=1, concat_axis=0, tiled=True
    )
    y_terms = operator_terms(open_edge(whole_conduct, 0, 0), 0, across_y)
    current = mixed
    for sweep in range(ITERS):
        current = line_solve(current, x_terms, 1, across_x)
        whole_lines = lax.all_to_all(
            to_lines(current, partners), "gy", split_axis=1, concat_axis=0, tiled=True
        )
        solved = line_solve(whole_lines, y_terms, 0, across_y)
        current = from_lines(
            lax.all_to_all(solved, "gy", split_axis=0, concat_axis=1, tiled=True), current.shape
        )
    return current


LANES = 128
SUBLANES = 8


def channels_fit(shape, fields, split_x, split_y):
    rows, span, width = shape
    return (
        span == SUBLANES
        and rows * span * split_x == LANES
        and fields == split_x
        and SUBLANES % split_x == 0
        and width == SUBLANES * split_x * split_y
        and rows & (rows - 1) == 0
        and split_x & (split_x - 1) == 0
        and split_y & (split_y - 1) == 0
    )


def cyclic_reduction(kleft, length, at, paired):
    excess = jnp.ones_like(kleft)
    west = kleft
    east = at(kleft, 1)
    levels = []
    stride = 1
    while stride < length:
        inverse = 1.0 / (excess + west + east)
        from_west = west * at(inverse, -stride)
        from_east = east * at(inverse, stride)
        excess = excess + from_west * at(excess, -stride) + from_east * at(excess, stride)
        west = from_west * at(west, -stride)
        east = from_east * at(east, stride)
        levels.append((stride, from_west, from_east))
        stride *= 2
    steps = []
    while levels:
        near, west_near, east_near = levels.pop(0)
        if levels and paired(near):
            far, west_far, east_far = levels.pop(0)
            steps.append(
                (
                    (-near, west_near + west_far * at(east_near, -far)),
                    (near, east_near + east_far * at(west_near, far)),
                    (-far, west_far),
                    (far, east_far),
                    (-near - far, west_far * at(west_near, -far)),
                    (near + far, east_far * at(east_near, far)),
                )
            )
        else:
            steps.append(((-near, west_near), (near, east_near)))
    return steps, 1.0 / excess


def reduced_solve(values, operator, at):
    steps, inverse = operator
    for taps in steps:
        terms = [coefficient * at(values, offset) for offset, coefficient in taps]
        terms = [first + second for first, second in zip(terms[::2], terms[1::2])]
        values = (values + terms[0]) + sum(terms[2:], terms[1]) if terms[1:] else values + terms[0]
    return values * inverse


def swap_blocks(values, span, split_x):
    row = lax.broadcasted_iota(jnp.int32, values.shape, 0)
    lane = lax.broadcasted_iota(jnp.int32, values.shape, 1)
    down, along = (SUBLANES // split_x, span)
    while down < SUBLANES:
        row_bit = (row // down) % 2
        lane_bit = (lane // along) % 2
        later = pltpu.roll(pltpu.roll(values, along, 1), values.shape[0] - down, 0)
        earlier = pltpu.roll(pltpu.roll(values, LANES - along, 1), down, 0)
        values = jnp.where(row_bit == lane_bit, values, jnp.where(lane_bit == 1, later, earlier))
        down, along = (down * 2, along * 2)
    return values


def channel_kernel(
    split_x,
    split_y,
    chi_hbm,
    sigma_hbm,
    vertical_hbm,
    kx_hbm,
    ky_hbm,
    out_ref,
    chi_ref,
    sigma_ref,
    vertical_ref,
    kx_ref,
    ky_ref,
    sent,
    got,
    solved,
    back,
    load_sems,
    sems,
    back_sems,
):
    rows, span, width = chi_ref.shape
    fields, levels, _ = vertical_ref.shape
    count = split_x * split_y
    length_x = split_x * span
    length_y = split_y * rows
    tall = split_y * SUBLANES
    gx, gy = (lax.axis_index("gx"), lax.axis_index("gy"))
    me = gy * split_x + gx

    loads = [
        pltpu.make_async_copy(source, target, load_sems.at[number])
        for number, (source, target) in enumerate(
            (
                (kx_hbm, kx_ref),
                (ky_hbm, ky_ref),
                (chi_hbm, chi_ref),
                (sigma_hbm, sigma_ref),
                (vertical_hbm, vertical_ref),
            )
        )
    ]
    for load in loads:
        load.start()

    partners_x = [lax.bitwise_xor(gx, jnp.int32(step)) for step in range(split_x)]
    partners_y = [lax.bitwise_xor(gy, jnp.int32(step)) for step in range(split_y)]
    partners = [
        (partners_x[step_x], partners_y[step_y])
        for step_y in reversed(range(split_y))
        for step_x in range(split_x)
        if step_x or step_y
    ]

    barrier = pltpu.get_barrier_semaphore()
    for peer_x, peer_y in partners:
        pl.semaphore_signal(
            barrier,
            inc=1,
            device_id={"gx": peer_x, "gy": peer_y},
            device_id_type=pl.DeviceIdType.MESH,
        )

    def send_all(source, target, sems):
        for peer_x, peer_y in partners:
            pltpu.make_async_remote_copy(
                src_ref=source(peer_y * split_x + peer_x),
                dst_ref=target(me),
                send_sem=sems.at[0],
                recv_sem=sems.at[1],
                device_id={"gx": peer_x, "gy": peer_y},
                device_id_type=pl.DeviceIdType.MESH,
            ).start()

    others = pl.ds(0, count - 1)
    loads[0].wait()
    loads[1].wait()
    group = width // split_x
    conducts = jnp.concatenate(
        [
            jnp.concatenate([ref[row][:, h * group : (h + 1) * group] for ref in (kx_ref, ky_ref)], 1)
            for row in range(rows)
            for h in range(split_x)
        ],
        0,
    )
    conducts = conducts.T.reshape((2,) + back.shape)
    sent[:, 0] = conducts[0]
    sent[:, 1] = conducts[1]

    for load in loads[2:]:
        load.wait()
    field_of = lax.broadcasted_iota(jnp.int32, (span, width), 1) // levels
    scaled = [sigma_ref[row] * chi_ref[row] for row in range(rows)]
    stacked = jnp.dot(
        jnp.concatenate(
            [jnp.where(field_of == f, scaled[row], 0.0) for row in range(rows) for f in range(fields)],
            0,
        ),
        vertical_ref[...].reshape(width, levels),
        precision=lax.Precision.HIGHEST,
        preferred_element_type=jnp.float32,
    )
    sent[:, 2] = stacked.T.reshape(back.shape)
    pl.semaphore_wait(barrier, count - 1)
    send_all(lambda at: sent.at[at], lambda at: got.at[at], sems)
    got[me] = sent[me]

    lane = lax.broadcasted_iota(jnp.int32, (tall, LANES), 1)
    tile_row = lax.broadcasted_iota(jnp.int32, (tall, LANES), 0)
    cell_x = lane % length_x

    def tiles_on(values, tiles_by):
        moved = (tiles_by % split_y) * SUBLANES
        if moved == 0:
            return values
        return jnp.concatenate([values[-moved:], values[:-moved]], 0)

    def at_x(values, offset):
        return pltpu.roll(values, (LANES - offset) % LANES, 1)

    def at_y(values, offset):
        if abs(offset) >= rows:
            return tiles_on(values, -offset // rows)
        lanes = offset * length_x
        turned_by = pltpu.roll(values, (LANES - lanes) % LANES, 1)
        if offset < 0:
            return jnp.where(lane < -lanes, tiles_on(turned_by, 1), turned_by)
        return jnp.where(lane >= LANES - lanes, tiles_on(turned_by, -1), turned_by)

    pltpu.make_async_copy(got.at[others], got.at[others], sems.at[1]).wait()
    west = swap_blocks(got[:, 0].reshape(tall, LANES), span, split_x)
    south = swap_blocks(got[:, 1].reshape(tall, LANES), span, split_x)
    west = jnp.where(cell_x == 0, 0.0, west)
    south = jnp.where((tile_row < SUBLANES) & (lane < length_x), 0.0, south)
    x_operator = cyclic_reduction(west, length_x, at_x, lambda near: 3 * near < length_x)
    y_operator = cyclic_reduction(south, length_y, at_y, lambda near: 3 * near < rows)
    field = swap_blocks(got[:, 2].reshape(tall, LANES), span, split_x)
    for sweep in range(ITERS):
        field = reduced_solve(field, x_operator, at_x)
        field = reduced_solve(field, y_operator, at_y)
    solved[...] = swap_blocks(field, span, split_x).reshape(solved.shape)
    send_all(lambda at: solved.at[at], lambda at: back.at[at], back_sems)
    back[me] = solved[me]
    pltpu.make_async_copy(back.at[others], back.at[others], back_sems.at[1]).wait()
    turned = back[...].reshape(tall, LANES).T
    for row in range(rows):
        out_ref[row] = jnp.concatenate(
            [
                turned[(row * split_x + h) * span : (row * split_x + h + 1) * span]
                for h in range(split_x)
            ],
            1,
        )
    pltpu.make_async_copy(sent.at[others], sent.at[others], sems.at[0]).wait()
    pltpu.make_async_copy(solved.at[others], solved.at[others], back_sems.at[0]).wait()


def channel_body(split_x, split_y, chi, sigma, vertical, kx, ky):
    count = split_x * split_y
    share = SUBLANES // split_x
    block = pltpu.VMEM(chi.shape, jnp.float32)
    packed = pltpu.VMEM((count, share, LANES), jnp.float32)
    packed_triple = pltpu.VMEM((count, 3, share, LANES), jnp.float32)
    return pl.pallas_call(
        functools.partial(channel_kernel, split_x, split_y),
        out_shape=pltpu.VMEM(chi.shape, jnp.float32),
        in_specs=[pl.BlockSpec(memory_space=pl.ANY)] * 5,
        out_specs=pl.BlockSpec(memory_space=pltpu.VMEM),
        scratch_shapes=[
            block,
            block,
            pltpu.VMEM(vertical.shape, jnp.float32),
            block,
            block,
            packed_triple,
            packed_triple,
            packed,
            packed,
            pltpu.SemaphoreType.DMA((5,)),
            pltpu.SemaphoreType.DMA((2,)),
            pltpu.SemaphoreType.DMA((2,)),
        ],
        compiler_params=pltpu.CompilerParams(collective_id=0, has_side_effects=True),
        name="channel_lines",
    )(chi, sigma, vertical, kx, ky)


def solution(mesh):
    split_x, split_y = (mesh.shape["gx"], mesh.shape["gy"])

    def chosen(chi, sigma, vertical, kx, ky):
        if channels_fit(chi.shape, vertical.shape[0], split_x, split_y):
            return channel_body(split_x, split_y, chi, sigma, vertical, kx, ky)
        return body(chi, sigma, vertical, kx, ky)


    placed = (
        P("gy", "gx", None),
        P("gy", "gx", None),
        P(),
        P("gy", "gx", None),
        P("gy", "gx", None),
    )
    return jax.shard_map(
        chosen, mesh=mesh, in_specs=placed, out_specs=P("gy", "gx", None), check_vma=False
    )
```

profile of v0, /device:TPU:0, one launch (start us, length us, event | category | flops | bytes accessed | tf_op | source)
XLA Modules:
  0.0 18.8 jit_solution(7535097326259334479)
XLA Ops:
  0.0 18.1 %channel_lines.1 = f32[4,8,256]{2,1,0:T(8,128)S(1)} custom-call(f32[4,8,256]{2,1,0:T(8,128)} %chi_hbm.1, f32[4,8,256]{2,1,0:T(8,128)} %sigma_hbm.1, f32[4,64,64]{2,1,0:T(8,128)} %vertical_hbm.1, f32[4,8,256]{2,1,0:T(8,128)} %kx_hbm.1, f32[4,8,256]{2,1,0:T(8,128)} %ky_hbm.1), custom_call_target="tpu_custom_call" | custom-call | tf_op jit(solution)/shard_map/channel_lines/pallas_call | solution.py:415
  18.1 0.6 %copy.7 = f32[4,8,256]{2,1,0:T(8,128)} copy(f32[4,8,256]{2,1,0:T(8,128)S(1)} %channel_lines.1) | data formatting | bytes 65536
where the time goes:
time: 18.9 us; the launch traced here: 18.8 us
  Pallas kernels  18.1 us (96%)
  local copies, waits for them, and re-layouts  0.62 us (3%)
    pallas_call x1, Pallas kernels, channel_body(): pl.pallas_call(functools.partial(channel_kernel, split_x, split_y), out_s...  18.1 us
    unnamed x1, local copies, waits for them, and re-layouts  0.62 us

commit v1 on v0

--- a/solution.py
+++ b/solution.py
@@ -234,17 +234,18 @@
 
 
 def swap_blocks(values, span, split_x):
-    row = lax.broadcasted_iota(jnp.int32, values.shape, 0)
-    lane = lax.broadcasted_iota(jnp.int32, values.shape, 1)
-    down, along = (SUBLANES // split_x, span)
-    while down < SUBLANES:
-        row_bit = (row // down) % 2
-        lane_bit = (lane // along) % 2
-        later = pltpu.roll(pltpu.roll(values, along, 1), values.shape[0] - down, 0)
-        earlier = pltpu.roll(pltpu.roll(values, LANES - along, 1), down, 0)
-        values = jnp.where(row_bit == lane_bit, values, jnp.where(lane_bit == 1, later, earlier))
-        down, along = (down * 2, along * 2)
-    return values
+    share = SUBLANES // split_x
+    tiles = values.reshape(-1, SUBLANES, LANES)
+    group = lax.broadcasted_iota(jnp.int32, tiles.shape, 1) // share
+    block = (lax.broadcasted_iota(jnp.int32, tiles.shape, 2) // span) % split_x
+    apart = (block - group + split_x) % split_x
+    swapped = tiles
+    for k in range(1, split_x):
+        ahead = pltpu.roll(tiles, span * k, 2)
+        wrapped = pltpu.roll(tiles, LANES - span * (split_x - k), 2)
+        moved = pltpu.roll(jnp.where(block >= k, ahead, wrapped), SUBLANES - share * k, 1)
+        swapped = jnp.where(apart == k, moved, swapped)
+    return swapped.reshape(values.shape)
 
 
 def channel_kernel(

time: 18.9 us -> 18.7 us (0.989)
  no operation moved by 1% of the time
where the time goes in v1:
time: 18.7 us; the launch traced here: 18.6 us
  Pallas kernels  18 us (96%)
  local copies, waits for them, and re-layouts  0.62 us (3%)
    pallas_call x1, Pallas kernels, channel_body(): pl.pallas_call(functools.partial(channel_kernel, split_x, split_y), out_s...  18 us
    unnamed x1, local copies, waits for them, and re-layouts  0.62 us

profile of v1, /device:TPU:0, one launch (start us, length us, event | category | flops | bytes accessed | tf_op | source)
XLA Modules:
  0.0 18.6 jit_solution(14303014115063136386)
XLA Ops:
  0.0 18.0 %channel_lines.1 = f32[4,8,256]{2,1,0:T(8,128)S(1)} custom-call(f32[4,8,256]{2,1,0:T(8,128)} %chi_hbm.1, f32[4,8,256]{2,1,0:T(8,128)} %sigma_hbm.1, f32[4,64,64]{2,1,0:T(8,128)} %vertical_hbm.1, f32[4,8,256]{2,1,0:T(8,128)} %kx_hbm.1, f32[4,8,256]{2,1,0:T(8,128)} %ky_hbm.1), custom_call_target="tpu_custom_call" | custom-call | tf_op jit(solution)/shard_map/channel_lines/pallas_call | solution.py:416
  18.0 0.6 %copy.7 = f32[4,8,256]{2,1,0:T(8,128)} copy(f32[4,8,256]{2,1,0:T(8,128)S(1)} %channel_lines.1) | data formatting | bytes 65536

commit v2 on v1

--- a/solution.py
+++ b/solution.py
@@ -294,17 +294,22 @@
     for load in loads:
         load.start()
 
-    partners_x = [lax.bitwise_xor(gx, jnp.int32(step)) for step in range(split_x)]
-    partners_y = [lax.bitwise_xor(gy, jnp.int32(step)) for step in range(split_y)]
-    partners = [
-        (partners_x[step_x], partners_y[step_y])
-        for step_y in reversed(range(split_y))
-        for step_x in range(split_x)
-        if step_x or step_y
-    ]
+    partners_x = [lax.bitwise_xor(gx, jnp.int32(step)) for step in reversed(range(split_x))]
+
+    def each_partner(act):
+        def line(number, _):
+            peer_y = lax.bitwise_xor(gy, split_y - 1 - number)
+            for peer_x in partners_x:
+                act(peer_x, peer_y)
+            return 0
+
+        lax.fori_loop(0, split_y - 1, line, 0)
+        for peer_x in partners_x[:-1]:
+            act(peer_x, gy)
 
     barrier = pltpu.get_barrier_semaphore()
-    for peer_x, peer_y in partners:
+
+    def greet(peer_x, peer_y):
         pl.semaphore_signal(
             barrier,
             inc=1,
@@ -312,8 +317,10 @@
             device_id_type=pl.DeviceIdType.MESH,
         )
 
+    each_partner(greet)
+
     def send_all(source, target, sems):
-        for peer_x, peer_y in partners:
+        def send(peer_x, peer_y):
             pltpu.make_async_remote_copy(
                 src_ref=source(peer_y * split_x + peer_x),
                 dst_ref=target(me),
@@ -322,6 +329,8 @@
                 device_id={"gx": peer_x, "gy": peer_y},
                 device_id_type=pl.DeviceIdType.MESH,
             ).start()
+
+        each_partner(send)
 
     others = pl.ds(0, count - 1)
     loads[0].wait()
@@ -387,9 +396,12 @@
     x_operator = cyclic_reduction(west, length_x, at_x, lambda near: 3 * near < length_x)
     y_operator = cyclic_reduction(south, length_y, at_y, lambda near: 3 * near < rows)
     field = swap_blocks(got[:, 2].reshape(tall, LANES), span, split_x)
-    for sweep in range(ITERS):
+
+    def sweep(number, field):
         field = reduced_solve(field, x_operator, at_x)
-        field = reduced_solve(field, y_operator, at_y)
+        return reduced_solve(field, y_operator, at_y)
+
+    field = lax.fori_loop(0, ITERS, sweep, field)
     solved[...] = swap_blocks(field, span, split_x).reshape(solved.shape)
     send_all(lambda at: solved.at[at], lambda at: back.at[at], back_sems)
     back[me] = solved[me]

time: 18.7 us -> 19.1 us (1.021)
  Pallas kernels: 18 us -> 18.3 us
    pallas_call x1, Pallas kernels: 18 us -> 18.3 us  [channel_body(): pl.pallas_call(functools.partial(channel_kernel, split_x, split_y), out_s...]
where the time goes in v2:
time: 19.1 us; the launch traced here: 19 us
  Pallas kernels  18.3 us (96%)
  local copies, waits for them, and re-layouts  0.62 us (3%)
    pallas_call x1, Pallas kernels, channel_body(): pl.pallas_call(functools.partial(channel_kernel, split_x, split_y), out_s...  18.3 us
    unnamed x1, local copies, waits for them, and re-layouts  0.62 us

profile of v2, /device:TPU:0, one launch (start us, length us, event | category | flops | bytes accessed | tf_op | source)
XLA Modules:
  0.0 19.0 jit_solution(10738293147085610498)
XLA Ops:
  0.0 18.3 %channel_lines.1 = f32[4,8,256]{2,1,0:T(8,128)S(1)} custom-call(f32[4,8,256]{2,1,0:T(8,128)} %chi_hbm.1, f32[4,8,256]{2,1,0:T(8,128)} %sigma_hbm.1, f32[4,64,64]{2,1,0:T(8,128)} %vertical_hbm.1, f32[4,8,256]{2,1,0:T(8,128)} %kx_hbm.1, f32[4,8,256]{2,1,0:T(8,128)} %ky_hbm.1), custom_call_target="tpu_custom_call" | custom-call | tf_op jit(solution)/shard_map/channel_lines/pallas_call | solution.py:428
  18.3 0.6 %copy.7 = f32[4,8,256]{2,1,0:T(8,128)} copy(f32[4,8,256]{2,1,0:T(8,128)S(1)} %channel_lines.1) | data formatting | bytes 65536

commit v3 on v1

--- a/solution.py
+++ b/solution.py
@@ -262,10 +262,10 @@
     vertical_ref,
     kx_ref,
     ky_ref,
-    sent,
-    got,
-    solved,
-    back,
+    sent_flat,
+    got_flat,
+    solved_flat,
+    back_flat,
     load_sems,
     sems,
     back_sems,
@@ -276,6 +276,9 @@
     length_x = split_x * span
     length_y = split_y * rows
     tall = split_y * SUBLANES
+    pieces = (count, SUBLANES // split_x, LANES)
+    sent, got = (flat.reshape((3,) + pieces) for flat in (sent_flat, got_flat))
+    solved, back = (flat.reshape(pieces) for flat in (solved_flat, back_flat))
     gx, gy = (lax.axis_index("gx"), lax.axis_index("gy"))
     me = gy * split_x + gx
 
@@ -335,9 +338,7 @@
         ],
         0,
     )
-    conducts = conducts.T.reshape((2,) + back.shape)
-    sent[:, 0] = conducts[0]
-    sent[:, 1] = conducts[1]
+    sent_flat[: 2 * tall] = conducts.T
 
     for load in loads[2:]:
         load.wait()
@@ -352,10 +353,11 @@
         precision=lax.Precision.HIGHEST,
         preferred_element_type=jnp.float32,
     )
-    sent[:, 2] = stacked.T.reshape(back.shape)
+    sent_flat[2 * tall :] = stacked.T
     pl.semaphore_wait(barrier, count - 1)
-    send_all(lambda at: sent.at[at], lambda at: got.at[at], sems)
-    got[me] = sent[me]
+    send_all(lambda at: sent.at[:, at], lambda at: got.at[:, at], sems)
+    mine = pltpu.make_async_copy(sent.at[:, me], got.at[:, me], load_sems.at[0])
+    mine.start()
 
     lane = lax.broadcasted_iota(jnp.int32, (tall, LANES), 1)
     tile_row = lax.broadcasted_iota(jnp.int32, (tall, LANES), 0)
@@ -379,22 +381,25 @@
             return jnp.where(lane < -lanes, tiles_on(turned_by, 1), turned_by)
         return jnp.where(lane >= LANES - lanes, tiles_on(turned_by, -1), turned_by)
 
-    pltpu.make_async_copy(got.at[others], got.at[others], sems.at[1]).wait()
-    west = swap_blocks(got[:, 0].reshape(tall, LANES), span, split_x)
-    south = swap_blocks(got[:, 1].reshape(tall, LANES), span, split_x)
+    pltpu.make_async_copy(got.at[:, others], got.at[:, others], sems.at[1]).wait()
+    mine.wait()
+    west = swap_blocks(got_flat[0 * tall : 1 * tall], span, split_x)
+    south = swap_blocks(got_flat[1 * tall : 2 * tall], span, split_x)
     west = jnp.where(cell_x == 0, 0.0, west)
     south = jnp.where((tile_row < SUBLANES) & (lane < length_x), 0.0, south)
     x_operator = cyclic_reduction(west, length_x, at_x, lambda near: 3 * near < length_x)
     y_operator = cyclic_reduction(south, length_y, at_y, lambda near: 3 * near < rows)
-    field = swap_blocks(got[:, 2].reshape(tall, LANES), span, split_x)
+    field = swap_blocks(got_flat[2 * tall : 3 * tall], span, split_x)
     for sweep in range(ITERS):
         field = reduced_solve(field, x_operator, at_x)
         field = reduced_solve(field, y_operator, at_y)
-    solved[...] = swap_blocks(field, span, split_x).reshape(solved.shape)
+    solved_flat[...] = swap_blocks(field, span, split_x)
     send_all(lambda at: solved.at[at], lambda at: back.at[at], back_sems)
-    back[me] = solved[me]
+    mine = pltpu.make_async_copy(solved.at[me], back.at[me], load_sems.at[0])
+    mine.start()
     pltpu.make_async_copy(back.at[others], back.at[others], back_sems.at[1]).wait()
-    turned = back[...].reshape(tall, LANES).T
+    mine.wait()
+    turned = back_flat[...].T
     for row in range(rows):
         out_ref[row] = jnp.concatenate(
             [
@@ -403,16 +408,15 @@
             ],
             1,
         )
-    pltpu.make_async_copy(sent.at[others], sent.at[others], sems.at[0]).wait()
+    pltpu.make_async_copy(sent.at[:, others], sent.at[:, others], sems.at[0]).wait()
     pltpu.make_async_copy(solved.at[others], solved.at[others], back_sems.at[0]).wait()
 
 
 def channel_body(split_x, split_y, chi, sigma, vertical, kx, ky):
-    count = split_x * split_y
-    share = SUBLANES // split_x
+    tall = split_y * SUBLANES
     block = pltpu.VMEM(chi.shape, jnp.float32)
-    packed = pltpu.VMEM((count, share, LANES), jnp.float32)
-    packed_triple = pltpu.VMEM((count, 3, share, LANES), jnp.float32)
+    packed = pltpu.VMEM((tall, LANES), jnp.float32)
+    packed_triple = pltpu.VMEM((3 * tall, LANES), jnp.float32)
     return pl.pallas_call(
         functools.partial(channel_kernel, split_x, split_y),
         out_shape=pltpu.VMEM(chi.shape, jnp.float32),

time: 18.7 us -> 18.7 us (level)
  no operation moved by 1% of the time
where the time goes in v3:
time: 18.7 us; the launch traced here: 18.6 us
  Pallas kernels  18 us (96%)
  local copies, waits for them, and re-layouts  0.62 us (3%)
    pallas_call x1, Pallas kernels, channel_body(): pl.pallas_call(functools.partial(channel_kernel, split_x, split_y), out_s...  18 us
    unnamed x1, local copies, waits for them, and re-layouts  0.62 us

profile of v3, /device:TPU:0, one launch (start us, length us, event | category | flops | bytes accessed | tf_op | source)
XLA Modules:
  0.0 18.6 jit_solution(4448042547119306178)
XLA Ops:
  0.0 18.0 %channel_lines.1 = f32[4,8,256]{2,1,0:T(8,128)S(1)} custom-call(f32[4,8,256]{2,1,0:T(8,128)} %chi_hbm.1, f32[4,8,256]{2,1,0:T(8,128)} %sigma_hbm.1, f32[4,64,64]{2,1,0:T(8,128)} %vertical_hbm.1, f32[4,8,256]{2,1,0:T(8,128)} %kx_hbm.1, f32[4,8,256]{2,1,0:T(8,128)} %ky_hbm.1), custom_call_target="tpu_custom_call" | custom-call | tf_op jit(solution)/shard_map/channel_lines/pallas_call | solution.py:420
  18.0 0.6 %copy.7 = f32[4,8,256]{2,1,0:T(8,128)} copy(f32[4,8,256]{2,1,0:T(8,128)S(1)} %channel_lines.1) | data formatting | bytes 65536

commit v4 on v3

--- a/solution.py
+++ b/solution.py
@@ -189,7 +189,7 @@
     )
 
 
-def cyclic_reduction(kleft, length, at, paired):
+def cyclic_reduction(kleft, length, at, paired, values):
     excess = jnp.ones_like(kleft)
     west = kleft
     east = at(kleft, 1)
@@ -203,7 +203,12 @@
         west = from_west * at(west, -stride)
         east = from_east * at(east, stride)
         levels.append((stride, from_west, from_east))
+        if values is not None:
+            values = values + (from_west * at(values, -stride) + from_east * at(values, stride))
         stride *= 2
+    inverse = 1.0 / excess
+    if values is not None:
+        values = values * inverse
     steps = []
     while levels:
         near, west_near, east_near = levels.pop(0)
@@ -221,7 +226,7 @@
             )
         else:
             steps.append(((-near, west_near), (near, east_near)))
-    return steps, 1.0 / excess
+    return (steps, inverse), values
 
 
 def reduced_solve(values, operator, at):
@@ -302,7 +307,7 @@
     partners = [
         (partners_x[step_x], partners_y[step_y])
         for step_y in reversed(range(split_y))
-        for step_x in range(split_x)
+        for step_x in reversed(range(split_x))
         if step_x or step_y
     ]
 
@@ -387,11 +392,14 @@
     south = swap_blocks(got_flat[1 * tall : 2 * tall], span, split_x)
     west = jnp.where(cell_x == 0, 0.0, west)
     south = jnp.where((tile_row < SUBLANES) & (lane < length_x), 0.0, south)
-    x_operator = cyclic_reduction(west, length_x, at_x, lambda near: 3 * near < length_x)
-    y_operator = cyclic_reduction(south, length_y, at_y, lambda near: 3 * near < rows)
     field = swap_blocks(got_flat[2 * tall : 3 * tall], span, split_x)
+    x_operator, field = cyclic_reduction(
+        west, length_x, at_x, lambda near: 3 * near < length_x, field
+    )
+    y_operator, _ = cyclic_reduction(south, length_y, at_y, lambda near: 3 * near < rows, None)
     for sweep in range(ITERS):
-        field = reduced_solve(field, x_operator, at_x)
+        if sweep:
+            field = reduced_solve(field, x_operator, at_x)
         field = reduced_solve(field, y_operator, at_y)
     solved_flat[...] = swap_blocks(field, span, split_x)
     send_all(lambda at: solved.at[at], lambda at: back.at[at], back_sems)

time: 18.7 us -> 18.6 us (level)
  no operation moved by 1% of the time
where the time goes in v4:
time: 18.6 us; the launch traced here: 18.5 us
  Pallas kernels  17.9 us (96%)
  local copies, waits for them, and re-layouts  0.62 us (3%)
    pallas_call x1, Pallas kernels, channel_body(): pl.pallas_call(functools.partial(channel_kernel, split_x, split_y), out_s...  17.9 us
    unnamed x1, local copies, waits for them, and re-layouts  0.62 us

profile of v4, /device:TPU:0, one launch (start us, length us, event | category | flops | bytes accessed | tf_op | source)
XLA Modules:
  0.0 18.5 jit_solution(11947734024409544356)
XLA Ops:
  0.0 17.9 %channel_lines.1 = f32[4,8,256]{2,1,0:T(8,128)S(1)} custom-call(f32[4,8,256]{2,1,0:T(8,128)} %chi_hbm.1, f32[4,8,256]{2,1,0:T(8,128)} %sigma_hbm.1, f32[4,64,64]{2,1,0:T(8,128)} %vertical_hbm.1, f32[4,8,256]{2,1,0:T(8,128)} %kx_hbm.1, f32[4,8,256]{2,1,0:T(8,128)} %ky_hbm.1), custom_call_target="tpu_custom_call" | custom-call | tf_op jit(solution)/shard_map/channel_lines/pallas_call | solution.py:428
  17.9 0.6 %copy.7 = f32[4,8,256]{2,1,0:T(8,128)} copy(f32[4,8,256]{2,1,0:T(8,128)S(1)} %channel_lines.1) | data formatting | bytes 65536

commit v5 on v1

--- a/solution.py
+++ b/solution.py
@@ -189,7 +189,7 @@
     )
 
 
-def cyclic_reduction(kleft, length, at, paired):
+def cyclic_reduction(kleft, length, at, paired, values):
     excess = jnp.ones_like(kleft)
     west = kleft
     east = at(kleft, 1)
@@ -203,7 +203,12 @@
         west = from_west * at(west, -stride)
         east = from_east * at(east, stride)
         levels.append((stride, from_west, from_east))
+        if values is not None:
+            values = values + (from_west * at(values, -stride) + from_east * at(values, stride))
         stride *= 2
+    inverse = 1.0 / excess
+    if values is not None:
+        values = values * inverse
     steps = []
     while levels:
         near, west_near, east_near = levels.pop(0)
@@ -221,7 +226,7 @@
             )
         else:
             steps.append(((-near, west_near), (near, east_near)))
-    return steps, 1.0 / excess
+    return (steps, inverse), values
 
 
 def reduced_solve(values, operator, at):
@@ -299,7 +304,7 @@
     partners = [
         (partners_x[step_x], partners_y[step_y])
         for step_y in reversed(range(split_y))
-        for step_x in range(split_x)
+        for step_x in reversed(range(split_x))
         if step_x or step_y
     ]
 
@@ -384,11 +389,14 @@
     south = swap_blocks(got[:, 1].reshape(tall, LANES), span, split_x)
     west = jnp.where(cell_x == 0, 0.0, west)
     south = jnp.where((tile_row < SUBLANES) & (lane < length_x), 0.0, south)
-    x_operator = cyclic_reduction(west, length_x, at_x, lambda near: 3 * near < length_x)
-    y_operator = cyclic_reduction(south, length_y, at_y, lambda near: 3 * near < rows)
     field = swap_blocks(got[:, 2].reshape(tall, LANES), span, split_x)
+    x_operator, field = cyclic_reduction(
+        west, length_x, at_x, lambda near: 3 * near < length_x, field
+    )
+    y_operator, _ = cyclic_reduction(south, length_y, at_y, lambda near: 3 * near < rows, None)
     for sweep in range(ITERS):
-        field = reduced_solve(field, x_operator, at_x)
+        if sweep:
+            field = reduced_solve(field, x_operator, at_x)
         field = reduced_solve(field, y_operator, at_y)
     solved[...] = swap_blocks(field, span, split_x).reshape(solved.shape)
     send_all(lambda at: solved.at[at], lambda at: back.at[at], back_sems)

time: 18.7 us -> 18.6 us (level)
  no operation moved by 1% of the time
where the time goes in v5:
time: 18.6 us; the launch traced here: 18.5 us
  Pallas kernels  17.9 us (96%)
  local copies, waits for them, and re-layouts  0.62 us (3%)
    pallas_call x1, Pallas kernels, channel_body(): pl.pallas_call(functools.partial(channel_kernel, split_x, split_y), out_s...  17.9 us
    unnamed x1, local copies, waits for them, and re-layouts  0.62 us

profile of v5, /device:TPU:0, one launch (start us, length us, event | category | flops | bytes accessed | tf_op | source)
XLA Modules:
  0.0 18.5 jit_solution(2426769737015843479)
XLA Ops:
  0.0 17.9 %channel_lines.1 = f32[4,8,256]{2,1,0:T(8,128)S(1)} custom-call(f32[4,8,256]{2,1,0:T(8,128)} %chi_hbm.1, f32[4,8,256]{2,1,0:T(8,128)} %sigma_hbm.1, f32[4,64,64]{2,1,0:T(8,128)} %vertical_hbm.1, f32[4,8,256]{2,1,0:T(8,128)} %kx_hbm.1, f32[4,8,256]{2,1,0:T(8,128)} %ky_hbm.1), custom_call_target="tpu_custom_call" | custom-call | tf_op jit(solution)/shard_map/channel_lines/pallas_call | solution.py:424
  17.9 0.6 %copy.7 = f32[4,8,256]{2,1,0:T(8,128)} copy(f32[4,8,256]{2,1,0:T(8,128)S(1)} %channel_lines.1) | data formatting | bytes 65536
